TPU v7x, 32 devices: a whole 2x2x4 slice. The times are simulated.
32 devices in a mesh: dp: 8 (over y, x, core), tensor: 4 (over z).
Axes of the slice: x: 2, y: 2, z: 4, core: 2. Of those that a mesh axis runs over, the one named last changes fastest.
Arguments:
- tokens: bfloat16 [2048, 4096], P('dp', 'tensor'), may hold values from -6 to 6
- weights: bfloat16 [512, 16, 4, 256], P(None, 'tensor'), may hold values from -0.25 to 0.25
- upstream: bfloat16 [2048, 4096], P('dp', 'tensor'), may hold values from -6 to 6
Outputs:
- activated: bfloat16 [2048, 4096], P('dp', 'tensor')
- token_grad: bfloat16 [2048, 4096], P('dp', 'tensor')
- weight_grad: float32 [512, 16, 4, 256], P('dp', 'tensor')
All inputs are finite; a program needn't handle non-finite values.
Results may differ from a plain program's by a relative error of at most 0.018.
Values may be sent and summed in bfloat16 or wider, within the bound.
A program may use at most 64 MiB of HBM per device.

v0:
```python
import math

import jax
import jax.numpy as jnp
from jax import lax
from jax.sharding import PartitionSpec as P

BLOCK_FEATURES = 256
FACTORS = 4


def partner_2(block, axis, stride):
    count = lax.axis_size(axis)
    route = []
    for low in range(count):
        high = low | 1 << stride
        if high != low and high < count:
            route += [(low, high), (high, low)]
    return lax.ppermute(block, axis, route)


def local_partner(values, distance):
    count, blocks, width = values.shape
    folded = values.reshape(count, blocks // (2 * distance), 2, distance, width)
    return folded[:, :, ::-1].reshape(count, blocks, width)


def level_of(distance, blocks):
    return (distance // blocks).bit_length() - 1


def forward_partner(values, distance):
    blocks = values.shape[1]
    if distance < blocks:
        return local_partner(values, distance)
    return partner_2(values, "tensor", level_of(distance, blocks))


def backward_partner(values, distance):
    blocks = values.shape[1]
    if distance < blocks:
        return local_partner(values, distance)
    return partner_2(values, "tensor", level_of(distance, blocks))


def again_partner(values, distance):
    blocks = values.shape[1]
    if distance < blocks:
        return local_partner(values, distance)
    return partner_2(values, "tensor", level_of(distance, blocks))


def grad_block(gathered_input, following_gradient, scale_factor):
    return scale_factor * jnp.einsum(
        "urs,urd->srd", gathered_input, following_gradient, preferred_element_type=jnp.float32
    )


def on_device(tokens, weights, upstream):
    tok_count = tokens.shape[0]
    blocks = tokens.shape[1] // BLOCK_FEATURES
    scale_factor = 1.0 / math.sqrt(tok_count * lax.axis_size("dp"))
    layer_number = tokens.reshape(tok_count, blocks, BLOCK_FEATURES)
    inputs_saved = []
    partners_saved = []
    for factor_matrix in range(FACTORS):
        partner = forward_partner(layer_number, 2**factor_matrix)
        inputs_saved.append(layer_number)
        partners_saved.append(partner)
        gathered_input = jnp.concatenate([layer_number, partner], axis=2)
        layer_number = jnp.einsum(
            "hjk,kjg->hjg",
            gathered_input,
            weights[:, :, factor_matrix, :],
            preferred_element_type=jnp.float32,
        ).astype(jnp.bfloat16)
    last = layer_number.astype(jnp.float32)
    activated = jax.nn.gelu(last).astype(jnp.bfloat16).reshape(tok_count, blocks * BLOCK_FEATURES)
    _, pull = jax.vjp(jax.nn.gelu, last)
    current_gradient = pull(
        upstream.reshape(tok_count, blocks, BLOCK_FEATURES).astype(jnp.float32)
    )[0].astype(jnp.bfloat16)
    joined_all = [None] * FACTORS
    grads_next = [None] * FACTORS
    for factor_matrix in reversed(range(FACTORS)):
        distance = 2**factor_matrix
        factor_weight = weights[:, :, factor_matrix, :]
        partner = again_partner(inputs_saved[factor_matrix], distance)
        gathered_input = jnp.concatenate([inputs_saved[factor_matrix], partner], axis=2)
        joined_all[factor_matrix] = gathered_input
        grads_next[factor_matrix] = current_gradient
        passed_input = jnp.einsum(
            "jvu,rvu->jvr",
            current_gradient,
            factor_weight[BLOCK_FEATURES:],
            preferred_element_type=jnp.float32,
        ).astype(jnp.bfloat16)
        self_portion = jnp.einsum(
            "jvu,rvu->jvr",
            current_gradient,
            factor_weight[:BLOCK_FEATURES],
            preferred_element_type=jnp.float32,
        )
        arrived = backward_partner(passed_input, distance)
        current_gradient = (self_portion + arrived.astype(jnp.float32)).astype(jnp.bfloat16)
    pieces = [
        grad_block(joined_all[factor_matrix], grads_next[factor_matrix], scale_factor)
        for factor_matrix in range(FACTORS)
    ]
    weight_grad = lax.psum_scatter(jnp.stack(pieces, axis=2), "dp", scatter_dimension=0, tiled=True)
    token_grad = current_gradient.reshape(tok_count, blocks * BLOCK_FEATURES)
    return (activated, token_grad, weight_grad)


def solution(mesh):
    placed = (P("dp", "tensor"), P(None, "tensor", None, None), P("dp", "tensor"))
    return jax.shard_map(
        on_device,
        mesh=mesh,
        in_specs=placed,
        out_specs=(P("dp", "tensor"), P("dp", "tensor"), P("dp", "tensor", None, None)),
        check_vma=False,
    )
```

profile of v0, /device:TPU:0, one launch (start us, length us, event | category | flops | bytes accessed | tf_op | source)
XLA Modules:
  0.0 288.1 jit_solution(7162826798101817281)
XLA Ops:
  7.2 1.4 reshape_reshape.4
  8.6 2.0 copy.66
  10.7 14.8 %fusion.32 = (bf16[512,4,1,256]{3,2,1,0:T(2,128)(2,1)}, bf16[512,4,1,256]{3,2,1,0:T(2,128)(2,1)}, bf16[512,4,1,256]{3,2,1,0:T(2,128)(2,1)}, bf16[512,4,1,256]{3,2,1,0:T(2,128)(2,1)S(1)}) fusion(bf16[512,4,4,256]{3,2,1,0:T(4,128)(2,1)} %param.4), kind=kLoop, calls=%fused_computation.66 | loop fusion | bytes 8388608 | tf_op jit(solution)/shard_map/slice | solution.py:74
  25.5 5.8 %copy.110 = bf16[512,4,1,256]{0,3,1,2:T(8,128)(2,1)} copy(bf16[512,4,1,256]{3,2,1,0:T(2,128)(2,1)} %get-tuple-element.21) | data formatting | bytes 2097152
  31.3 5.9 %copy.111 = bf16[512,4,1,256]{0,3,1,2:T(8,128)(2,1)} copy(bf16[512,4,1,256]{3,2,1,0:T(2,128)(2,1)} %get-tuple-element.20) | data formatting | bytes 2097152
  37.2 0.1 copy.67
  37.3 1.4 copy.68
  38.8 2.7 convolution_convert_fusion.7
  41.5 1.1 rev.15
  42.6 2.0 fusion.8
  44.6 3.1 %collective-permute-start = (bf16[256,4,256]{0,2,1:T(8,128)(2,1)S(1)}, bf16[256,4,256]{0,2,1:T(8,128)(2,1)}, u32[]{:S(2)}, u32[]{:S(2)}) collective-permute-start(bf16[256,4,256]{0,2,1:T(8,128)(2,1)S(1)} %fusion.8), channel_id=1, source_target_pairs={{0,1},{1,0},{2,3},{3,2},{4,5},{5,4},{6,7},{7,6},{8,9},{9,8},{10,11... | collective-permute-start | bytes 1572872 | tf_op jit(solution)/shard_map/ppermute | solution.py:19
  47.7 5.8 %copy.109 = bf16[512,4,1,256]{0,3,1,2:T(8,128)(2,1)} copy(bf16[512,4,1,256]{3,2,1,0:T(2,128)(2,1)} %get-tuple-element.22) | data formatting | bytes 2097152
  53.5 6.2 %collective-permute-done = bf16[256,4,256]{0,2,1:T(8,128)(2,1)} collective-permute-done((bf16[256,4,256]{0,2,1:T(8,128)(2,1)S(1)}, bf16[256,4,256]{0,2,1:T(8,128)(2,1)}, u32[]{:S(2)}, u32[]{:S(2)}) %collective-permute-start) | collective-permute-done | bytes 524320 | tf_op jit(solution)/shard_map/ppermute | solution.py:19
  59.7 2.6 fusion.9
  62.3 2.8 collective-permute-start.1
  65.0 16.0 %fusion.31 = (bf16[256,4,1,256]{3,2,1,0:T(2,128)(2,1)}, bf16[256,4,1,256]{3,2,1,0:T(2,128)(2,1)}, bf16[256,4,1,256]{3,2,1,0:T(2,128)(2,1)}, bf16[256,4,1,256]{3,...) fusion(bf16[512,4,4,256]{3,2,1,0:T(4,128)(2,1)} %param.4), kind=kLoop, calls=%fused_computation.65 | loop fusion | bytes 8388608 | tf_op jit(solution)/shard_map/slice | solution.py:101
  81.1 2.2 copy.76
  83.3 4.2 %copy.108 = bf16[512,4,1,256]{0,3,1,2:T(8,128)(2,1)} copy(bf16[512,4,1,256]{3,2,1,0:T(2,128)(2,1)S(1)} %get-tuple-element.23) | data formatting | bytes 2097152
  87.5 0.3 collective-permute-done.1
  87.8 3.8 %fusion.18 = (bf16[256,4,256]{0,2,1:T(8,128)(2,1)S(1)}, bf16[256,4,256]{0,2,1:T(8,128)(2,1)}) fusion(f32[256,4,256]{0,2,1:T(8,128)} %bitcast.133, bf16[256,4,256]{0,2,1:T(8,128)(2,1)} %collective-permute-done.1, bf16[256,4,256]{0,2,1:T(8,128)(2,1)} %fusion.9, bf16[512,4,1,256]{0,3,1,2:T(8,128)(2,1)} %copy.108), kind=kOutput, calls=%fused_computation.37 | convolution fusion | flops 276824064 | bytes 4194304 | tf_op jit(solution)/shard_map/hjk,kjg->hjg/dot_general | solution.py:71
  91.7 0.4 fusion.10
  92.0 0.1 collective-permute-start.2
  92.1 25.0 %collective-permute-done.2 = bf16[256,4,256]{2,0,1:T(8,128)(2,1)S(1)} collective-permute-done((bf16[256,4,256]{2,0,1:T(8,128)(2,1)S(1)}, bf16[256,4,256]{2,0,1:T(8,128)(2,1)S(1)}, u32[]{:S(2)}, u32[]{:S(2)}) %collective-permute-start.2) | collective-permute-done | bytes 524320 | tf_op jit(solution)/shard_map/ppermute | solution.py:19
  117.2 0.4 add_convert_fusion
  117.5 0.4 fusion.11
  117.9 0.1 collective-permute-start.3
  118.0 1.7 multiply_bitcast_fusion
  119.8 3.0 %multiply_bitcast_fusion.1 = f32[512,4,1,256]{0,3,1,2:T(8,128)} fusion(bf16[256,4,256]{2,0,1:T(8,128)(2,1)S(1)} %add_convert_fusion, bf16[256,4,256]{0,2,1:T(8,128)(2,1)} %collective-permute-done, bf16[256,4,256]{0,2,1:T(8,128)(2,1)S(1)} %copy-done.14), kind=kOutput, calls=%fused_computation.2 | convolution fusion | flops 271056896 | bytes 3670016 | tf_op jit(solution)/shard_map/urs,urd->srd/dot_general | solution.py:54
  122.8 7.4 %collective-permute-done.3 = bf16[256,4,256]{2,0,1:T(8,128)(2,1)S(1)} collective-permute-done((bf16[256,4,256]{2,0,1:T(8,128)(2,1)S(1)}, bf16[256,4,256]{2,0,1:T(8,128)(2,1)S(1)}, u32[]{:S(2)}, u32[]{:S(2)}) %collective-permute-start.3) | collective-permute-done | bytes 524320 | tf_op jit(solution)/shard_map/ppermute | solution.py:19
  130.1 0.4 fusion.3
  130.5 1.8 multiply_bitcast_fusion.2
  132.4 0.4 convolution_convert_fusion.1
  132.7 0.8 rev.16
  133.6 1.9 fusion.4
  135.4 1.8 multiply_bitcast_fusion.3
  137.3 0.1 copy-done
  137.4 4.0 %pad_maximum_fusion = f32[512,4,4,256]{0,3,1,2:T(8,128)} fusion(f32[512,4,1,256]{0,3,1,2:T(8,128)S(1)} %multiply_bitcast_fusion, f32[512,4,1,256]{0,3,1,2:T(8,128)S(1)} %copy-done, f32[512,4,1,256]{0,3,1,2:T(8,128)S(1)} %copy-done.1, f32[512,4,1,256]{0,3,1,2:T(8,128)S(1)} %multiply_bitcast_fusion.3), kind=kLoop, calls=%fused_computation | loop fusion | flops 6291456 | bytes 16777216 | tf_op jit(solution)/shard_map/stack | solution.py:110
  141.4 10.5 %copy.94 = f32[512,4,4,256]{3,2,1,0:T(4,128)} copy(f32[512,4,4,256]{0,3,1,2:T(8,128)} %pad_maximum_fusion) | data formatting | bytes 16777216 | tf_op jit(solution)/shard_map/stack | solution.py:110
  151.9 0.6 copy-done.16
  152.5 0.6 dynamic-slice
  153.8 1.0 copy.95
  154.8 0.4 convolution_convert_fusion
  155.2 0.2 copy.87
  155.4 0.6 copy-done.5
  156.0 0.4 fusion.5
  156.4 1.0 copy.96
  157.4 121.5 %all-reduce.3.cloned.1.call-done = f32[512,4,4,256]{3,2,1,0:T(4,128)} async-done(((f32[512,4,4,256]{3,2,1,0:T(4,128)}), f32[512,4,4,256]{3,2,1,0:T(4,128)}) %all-reduce.3.cloned.1.call-update) | async-done | bytes 8388624
  278.9 2.4 constant_dynamic-slice_fusion
  (35 shorter events, 0.2 us)
Async XLA Ops:
  7.2 271.7 %all-reduce.3.cloned.1.call-start = ((), (), s32[]{:S(2)}) async-start(), calls=%async_computation | async-start | bytes 16777216
  37.3 4.1 %copy-start.8 = (bf16[256,2,2,1,256]{4,0,2,1,3:T(8,128)(2,1)}, bf16[256,2,2,1,256]{4,0,2,1,3:T(8,128)(2,1)S(1)}, u32[]{:S(2)}) copy-start(bf16[256,2,2,1,256]{4,0,2,1,3:T(8,128)(2,1)S(1)} %rev.14) | copy-start | bytes 1572868
  38.8 3.8 %copy-start.9 = (bf16[256,4,256]{2,0,1:T(8,128)(2,1)}, bf16[256,4,256]{2,0,1:T(8,128)(2,1)S(1)}, u32[]{:S(2)}) copy-start(bf16[256,4,256]{2,0,1:T(8,128)(2,1)S(1)} %copy.68) | copy-start | bytes 1572868
  42.6 10.9 %copy-start.11 = (bf16[256,1,2,2,256]{0,4,3,2,1:T(8,128)(2,1)}, bf16[256,1,2,2,256]{0,4,3,2,1:T(8,128)(2,1)S(1)}, u32[]{:S(2)}) copy-start(bf16[256,1,2,2,256]{0,4,3,2,1:T(8,128)(2,1)S(1)} %rev.15) | copy-start | bytes 1572868
  44.6 17.7 %copy-start.13 = (bf16[256,4,256]{0,2,1:T(8,128)(2,1)}, bf16[256,4,256]{0,2,1:T(8,128)(2,1)S(1)}, u32[]{:S(2)}) copy-start(bf16[256,4,256]{0,2,1:T(8,128)(2,1)S(1)} %fusion.8) | copy-start | bytes 1572868
  44.6 15.1 %collective-permute-start = (bf16[256,4,256]{0,2,1:T(8,128)(2,1)S(1)}, bf16[256,4,256]{0,2,1:T(8,128)(2,1)}, u32[]{:S(2)}, u32[]{:S(2)}) collective-permute-start(bf16[256,4,256]{0,2,1:T(8,128)(2,1)S(1)} %fusion.8), channel_id=1, source_target_pairs={{0,1},{1,0},{2,3},{3,2},{4,5},{5,4},{6,7},{7,6},{8,9},{9,8},{10,11... | collective-permute-start | bytes 1572872 | tf_op jit(solution)/shard_map/ppermute | solution.py:19
  62.3 25.6 %collective-permute-start.1 = (bf16[256,4,256]{0,2,1:T(8,128)(2,1)}, bf16[256,4,256]{0,2,1:T(8,128)(2,1)}, u32[]{:S(2)}, u32[]{:S(2)}) collective-permute-start(bf16[256,4,256]{0,2,1:T(8,128)(2,1)} %fusion.9), channel_id=1, source_target_pairs={{0,2},{2,0},{1,3},{3,1},{4,6},{6,4},{5,7},{7,5},{8,10},{10,8},{9,1... | collective-permute-start | bytes 1572872 | tf_op jit(solution)/shard_map/ppermute | solution.py:19
  87.8 3.8 %copy-start.4 = (bf16[256,4,1,256]{3,2,1,0:T(2,128)(2,1)S(1)}, bf16[256,4,1,256]{3,2,1,0:T(2,128)(2,1)}, u32[]{:S(2)}) copy-start(bf16[256,4,1,256]{3,2,1,0:T(2,128)(2,1)} %get-tuple-element.17) | copy-start | bytes 1572868
  87.8 29.3 %copy-start.7 = (bf16[256,4,1,256]{3,2,1,0:T(2,128)(2,1)S(1)}, bf16[256,4,1,256]{3,2,1,0:T(2,128)(2,1)}, u32[]{:S(2)}) copy-start(bf16[256,4,1,256]{3,2,1,0:T(2,128)(2,1)} %get-tuple-element.18) | copy-start | bytes 1572868
  92.0 25.1 %collective-permute-start.2 = (bf16[256,4,256]{2,0,1:T(8,128)(2,1)S(1)}, bf16[256,4,256]{2,0,1:T(8,128)(2,1)S(1)}, u32[]{:S(2)}, u32[]{:S(2)}) collective-permute-start(bf16[256,4,256]{2,0,1:T(8,128)(2,1)S(1)} %fusion.10), channel_id=1, source_target_pairs={{0,2},{2,0},{1,3},{3,1},{4,6},{6,4},{5,7},{7,5},{8,10},{10,8},{9,1... | collective-permute-start | bytes 1572872 | tf_op jit(solution)/shard_map/ppermute | solution.py:19
  117.9 1.8 copy-start.14
  117.9 12.2 %collective-permute-start.3 = (bf16[256,4,256]{2,0,1:T(8,128)(2,1)S(1)}, bf16[256,4,256]{2,0,1:T(8,128)(2,1)S(1)}, u32[]{:S(2)}, u32[]{:S(2)}) collective-permute-start(bf16[256,4,256]{2,0,1:T(8,128)(2,1)S(1)} %fusion.11), channel_id=1, source_target_pairs={{0,1},{1,0},{2,3},{3,2},{4,5},{5,4},{6,7},{7,6},{8,9},{9,8},{10,11... | collective-permute-start | bytes 1572872 | tf_op jit(solution)/shard_map/ppermute | solution.py:19
  119.7 10.4 %copy-start.6 = (bf16[256,4,1,256]{3,2,1,0:T(2,128)(2,1)S(1)}, bf16[256,4,1,256]{3,2,1,0:T(2,128)(2,1)}, u32[]{:S(2)}) copy-start(bf16[256,4,1,256]{3,2,1,0:T(2,128)(2,1)} %get-tuple-element.16) | copy-start | bytes 1572868
  119.7 10.8 %copy-start.10 = (bf16[4,256,256]{1,2,0:T(8,128)(2,1)S(1)}, bf16[4,256,256]{1,2,0:T(8,128)(2,1)}, u32[]{:S(2)}) copy-start(bf16[4,256,256]{1,2,0:T(8,128)(2,1)} %convolution_convert_fusion.7) | copy-start | bytes 1572868
  119.8 10.8 %copy-start.12 = (bf16[256,1,2,2,256]{0,4,3,2,1:T(8,128)(2,1)S(1)}, bf16[256,1,2,2,256]{0,4,3,2,1:T(8,128)(2,1)}, u32[]{:S(2)}) copy-start(bf16[256,1,2,2,256]{0,4,3,2,1:T(8,128)(2,1)} %copy-done.11) | copy-start | bytes 1572868
  130.5 1.8 copy-start.3
  133.5 3.7 %copy-start.1 = (f32[512,4,1,256]{0,3,1,2:T(8,128)S(1)}, f32[512,4,1,256]{0,3,1,2:T(8,128)}, u32[]{:S(2)}) copy-start(f32[512,4,1,256]{0,3,1,2:T(8,128)} %multiply_bitcast_fusion.2) | copy-start | bytes 6291460
  135.4 2.0 copy-start
  151.9 0.7 copy-start.16
  151.9 1.9 copy-start.15
  151.9 2.9 %copy-start.2 = (bf16[256,4,1,256]{3,2,1,0:T(2,128)(2,1)S(1)}, bf16[256,4,1,256]{3,2,1,0:T(2,128)(2,1)}, u32[]{:S(2)}) copy-start(bf16[256,4,1,256]{3,2,1,0:T(2,128)(2,1)} %get-tuple-element.19) | copy-start | bytes 1572868
  154.8 1.2 copy-start.5
Sparse Core Ops, SparseCore 0:
  152.0 126.7 all-reduce.2
where the time goes:
time: 289 us; the launch traced here: 288 us
  waiting for transfers between devices  160 us (55%)
  local copies, waits for them, and re-layouts  78.8 us (27%)
  matrix products  23.9 us (8%)
  between operations  15 us (5%)
  starting transfers between devices  6.02 us (2%)
  other arithmetic  4.02 us (1%)
    unnamed x2, waiting for transfers between devices  122 us
    ppermute x4, waiting for transfers between devices, partner_2(): return lax.ppermute(block, axis, route)  38.9 us
    unnamed x43, local copies, waits for them, and re-layouts  30.1 us
    slice x1, local copies, waits for them, and re-layouts, on_device(): factor_weight[:BLOCK_FEATURES]  16 us
    slice x1, local copies, waits for them, and re-layouts, on_device(): weights[:, :, factor_matrix, :]  14.8 us
    dot_general x4, matrix products, on_device(): jnp.einsum('hjk,kjg->hjg', gathered_input, weights[:, :, factor_matrix, :...  11.1 us
    another operation x1, local copies, waits for them, and re-layouts, on_device(): jnp.stack(pieces, axis=2)  10.5 us
    dot_general x4, matrix products, grad_block(): jnp.einsum('urs,urd->srd', gathered_input, following_gradient, preferred_...  8.39 us
  transfers between devices with their start and end apart: 5, of which 5 were waited for; matrix products, arithmetic and copies ran while one was open for 13% of the time, Pallas kernels for 0%

commit v1 on v0

--- a/solution.py
+++ b/solution.py
@@ -1,8 +1,11 @@
+import functools
 import math
 
 import jax
 import jax.numpy as jnp
 from jax import lax
+from jax.experimental import pallas as pl
+from jax.experimental.pallas import tpu as pltpu
 from jax.sharding import PartitionSpec as P
 
 BLOCK_FEATURES = 256
@@ -56,7 +59,7 @@
     )
 
 
-def on_device(tokens, weights, upstream):
+def plain_device(tokens, weights, upstream):
     tok_count = tokens.shape[0]
     blocks = tokens.shape[1] // BLOCK_FEATURES
     scale_factor = 1.0 / math.sqrt(tok_count * lax.axis_size("dp"))
@@ -112,6 +115,340 @@
     return (activated, token_grad, weight_grad)
 
 
+CHUNKS = 4
+MESH = pl.DeviceIdType.MESH
+W = BLOCK_FEATURES
+NN = (((1,), (0,)), ((), ()))
+NT = (((1,), (1,)), ((), ()))
+TN = (((0,), (0,)), ((), ()))
+GELU_A = 0.7978845608
+GELU_B = 0.044715
+
+
+def dot(a, b, dims):
+    return lax.dot_general(a, b, dims, preferred_element_type=jnp.float32)
+
+
+def flip(index, bit):
+    return index + bit - 2 * bit * (lax.rem(index // bit, 2))
+
+
+def fused_kernel(
+    scale_factor,
+    tok_ref,
+    up_ref,
+    w_hbm,
+    act_out,
+    tg_out,
+    wg_out,
+    w,
+    z,
+    part,
+    grad,
+    hand,
+    hand_in,
+    self_part,
+    act,
+    tgrad,
+    wg,
+    wg_core,
+    wg_sum,
+    wg_in,
+    wg_fin,
+    w_sem,
+    out_sem,
+    z_send,
+    z_recv,
+    core_send,
+    core_recv,
+    chip_send,
+    chip_recv,
+):
+    rows = tok_ref.shape[0]
+    blocks = tok_ref.shape[1] // W
+    step = rows // CHUNKS
+    shard = wg_fin.shape[2]
+    dp = lax.axis_index("dp")
+    tensor = lax.axis_index("tensor")
+    core = lax.rem(dp, 2)
+    chip = dp // 2
+
+    loads = []
+    for k in range(FACTORS):
+        load = pltpu.make_async_copy(w_hbm.at[k], w.at[k], w_sem.at[k])
+        load.start()
+        loads.append(load)
+
+    near = (dp, flip(tensor, 1))
+    far = (dp, flip(tensor, 2))
+    sibling = (flip(dp, 1), tensor)
+    chips = [flip(chip, 1), flip(chip, 2), 3 - chip]
+    others = [(2 * c + core, tensor) for c in chips]
+
+    barrier = pltpu.get_barrier_semaphore()
+    for device in [near, far, sibling] + others:
+        pl.semaphore_signal(barrier, inc=1, device_id=device, device_id_type=MESH)
+    pl.semaphore_wait(barrier, 6)
+
+    def span(c):
+        return slice(c * step, (c + 1) * step)
+
+    def col(i):
+        return slice(i * W, (i + 1) * W)
+
+    def z_copy(stage, c):
+        src = (z.at[2], z.at[3], hand.at[1], hand.at[0])[stage]
+        dst = (part.at[0], part.at[1], hand_in.at[1], hand_in.at[0])[stage]
+        return pltpu.make_async_remote_copy(
+            src_ref=src.at[pl.ds(c * step, step)],
+            dst_ref=dst.at[pl.ds(c * step, step)],
+            send_sem=z_send.at[stage, c],
+            recv_sem=z_recv.at[stage, c],
+            device_id=(near, far, far, near)[stage],
+            device_id_type=MESH,
+        )
+
+    def z_value(k, c, i):
+        if k == 0:
+            return tok_ref[span(c), col(i)]
+        return z[k, span(c), col(i)]
+
+    def partner_value(k, c, i):
+        if k < 2:
+            return z_value(k, c, i ^ (1 << k))
+        return part[k - 2, span(c), col(i)]
+
+    def factor(k, c, i):
+        return dot(z_value(k, c, i), w[k, i, :W, :], NN) + dot(
+            partner_value(k, c, i), w[k, i, W:, :], NN
+        )
+
+    def stage_f1(c):
+        for k in range(2):
+            if c == 0:
+                loads[k].wait()
+            for i in range(blocks):
+                z[k + 1, span(c), col(i)] = factor(k, c, i).astype(jnp.bfloat16)
+        z_copy(0, c).start()
+
+    def stage_f2(c):
+        if c == 0:
+            loads[2].wait()
+        z_copy(0, c).wait_recv()
+        for i in range(blocks):
+            z[3, span(c), col(i)] = factor(2, c, i).astype(jnp.bfloat16)
+        z_copy(1, c).start()
+
+    def stage_f3(c):
+        if c == 0:
+            loads[3].wait()
+        z_copy(1, c).wait_recv()
+        for i in range(blocks):
+            v = factor(3, c, i).astype(jnp.bfloat16).astype(jnp.float32)
+            square = v * v
+            t = jnp.tanh(GELU_A * (v + GELU_B * (v * square)))
+            half = 0.5 * (1.0 + t)
+            act[span(c), col(i)] = (v * half).astype(jnp.bfloat16)
+            slope = half + (0.5 * v) * (1.0 - t * t) * (GELU_A * (1.0 + 3.0 * GELU_B * square))
+            g = (up_ref[span(c), col(i)].astype(jnp.float32) * slope).astype(jnp.bfloat16)
+            grad[3, span(c), col(i)] = g
+            hand[1, span(c), col(i)] = dot(g, w[3, i, W:, :], NT).astype(jnp.bfloat16)
+        z_copy(2, c).start()
+        for i in range(blocks):
+            self_part[1, span(c), col(i)] = dot(grad[3, span(c), col(i)], w[3, i, :W, :], NT)
+
+    def stage_b3(c):
+        z_copy(2, c).wait_recv()
+        for i in range(blocks):
+            g = self_part[1, span(c), col(i)] + hand_in[1, span(c), col(i)].astype(jnp.float32)
+            g = g.astype(jnp.bfloat16)
+            grad[2, span(c), col(i)] = g
+            hand[0, span(c), col(i)] = dot(g, w[2, i, W:, :], NT).astype(jnp.bfloat16)
+        z_copy(3, c).start()
+        for i in range(blocks):
+            self_part[0, span(c), col(i)] = dot(grad[2, span(c), col(i)], w[2, i, :W, :], NT)
+
+    def stage_b2(c):
+        z_copy(3, c).wait_recv()
+        for i in range(blocks):
+            g = self_part[0, span(c), col(i)] + hand_in[0, span(c), col(i)].astype(jnp.float32)
+            grad[1, span(c), col(i)] = g.astype(jnp.bfloat16)
+        for k in (1, 0):
+            both = [dot(grad[k, span(c), col(i)], w[k, i], NT) for i in range(blocks)]
+            for i in range(blocks):
+                handed = both[i ^ (1 << k)][:, W:].astype(jnp.bfloat16).astype(jnp.float32)
+                g = (both[i][:, :W] + handed).astype(jnp.bfloat16)
+                if k == 1:
+                    grad[0, span(c), col(i)] = g
+                else:
+                    tgrad[span(c), col(i)] = g
+
+    def core_copy(k):
+        return pltpu.make_async_remote_copy(
+            src_ref=wg.at[k, 1 - core],
+            dst_ref=wg_core.at[k],
+            send_sem=core_send.at[k],
+            recv_sem=core_recv.at[k],
+            device_id=sibling,
+            device_id_type=MESH,
+        )
+
+    def chip_copy(k, m):
+        return pltpu.make_async_remote_copy(
+            src_ref=wg_sum.at[k, chips[m]],
+            dst_ref=wg_in.at[k, m],
+            send_sem=chip_send.at[k, m],
+            recv_sem=chip_recv.at[k, m],
+            device_id=others[m],
+            device_id_type=MESH,
+        )
+
+    def weight_terms(k):
+        per = W // shard
+        for i in range(blocks):
+            g = grad[k, :, col(i)]
+            if k == 0:
+                lefts = (tok_ref[:, col(i)], tok_ref[:, col(i ^ 1)])
+            elif k == 1:
+                lefts = (z[1, :, col(i)], z[1, :, col(i ^ 2)])
+            else:
+                lefts = (z[k, :, col(i)], part[k - 2, :, col(i)])
+            for side in range(2):
+                total = dot(lefts[side], g, TN).astype(jnp.bfloat16)
+                for j in range(per):
+                    at = side * per + j
+                    wg[k, at % 2, at // 2, i] = total[j * shard : (j + 1) * shard]
+        core_copy(k).start()
+
+    def weight_sum(k):
+        core_copy(k).wait_recv()
+        for c in range(4):
+            wg_sum[k, c] = (
+                wg[k, core, c].astype(jnp.float32) + wg_core[k, c].astype(jnp.float32)
+            ).astype(jnp.bfloat16)
+        for m in (2, 0, 1):
+            chip_copy(k, m).start()
+
+    def weight_final(k):
+        total = wg_sum[k, chip].astype(jnp.float32)
+        for m in range(3):
+            chip_copy(k, m).wait_recv()
+            total = total + wg_in[k, m].astype(jnp.float32)
+        wg_fin[k] = total * scale_factor
+        copy = pltpu.make_async_copy(wg_fin.at[k], wg_out.at[k], out_sem.at[2 + k])
+        copy.start()
+        return copy
+
+    last = CHUNKS - 1
+    work = []
+    skew = 2
+    for stage, run in enumerate((stage_f1, stage_f2, stage_f3, stage_b3, stage_b2)):
+        for c in range(CHUNKS):
+            work.append((c + skew * stage, -stage, functools.partial(run, c)))
+    outs = []
+
+    def store_act():
+        outs.append(pltpu.make_async_copy(act, act_out, out_sem.at[0]))
+        outs[-1].start()
+
+    def store_tgrad():
+        outs.append(pltpu.make_async_copy(tgrad, tg_out, out_sem.at[1]))
+        outs[-1].start()
+
+    work.append((last + skew * 2, 1, store_act))
+    work.append((last + skew * 2, 2, lambda: weight_terms(3)))
+    work.append((last + skew * 2 + 1, 1, lambda: weight_sum(3)))
+    work.append((last + skew * 3, 1, lambda: weight_terms(2)))
+    work.append((last + skew * 3 + 1, 1, lambda: weight_sum(2)))
+    for _, _, run in sorted(work, key=lambda item: item[:2]):
+        run()
+    weight_terms(1)
+    weight_terms(0)
+    store_tgrad()
+    weight_sum(1)
+    weight_sum(0)
+    for k in (3, 2, 1, 0):
+        outs.append(weight_final(k))
+    for stage in range(4):
+        for c in range(CHUNKS):
+            z_copy(stage, c).wait_send()
+    for k in range(FACTORS):
+        core_copy(k).wait_send()
+        for m in range(3):
+            chip_copy(k, m).wait_send()
+    for copy in outs:
+        copy.wait()
+
+
+def fused_device(tokens, weights, upstream):
+    rows, width = tokens.shape
+    blocks = width // W
+    dp = lax.axis_size("dp")
+    shard = 2 * W // dp
+    scale_factor = 1.0 / math.sqrt(rows * dp)
+    w = weights.transpose(2, 1, 0, 3)
+    bf16, f32 = jnp.bfloat16, jnp.float32
+    dma = pltpu.SemaphoreType.DMA
+    whole = pltpu.VMEM((rows, width), bf16)
+    activated, token_grad, weight_grad = pl.pallas_call(
+        functools.partial(fused_kernel, scale_factor),
+        out_shape=(
+            jax.ShapeDtypeStruct((rows, width), bf16),
+            jax.ShapeDtypeStruct((rows, width), bf16),
+            jax.ShapeDtypeStruct((FACTORS, blocks, shard, W), f32),
+        ),
+        in_specs=[
+            pl.BlockSpec(memory_space=pltpu.VMEM),
+            pl.BlockSpec(memory_space=pltpu.VMEM),
+            pl.BlockSpec(memory_space=pl.ANY),
+        ],
+        out_specs=[pl.BlockSpec(memory_space=pl.ANY)] * 3,
+        scratch_shapes=[
+            pltpu.VMEM((FACTORS, blocks, 2 * W, W), bf16),
+            pltpu.VMEM((4, rows, width), bf16),
+            pltpu.VMEM((2, rows, width), bf16),
+            pltpu.VMEM((4, rows, width), bf16),
+            pltpu.VMEM((2, rows, width), bf16),
+            pltpu.VMEM((2, rows, width), bf16),
+            pltpu.VMEM((2, rows, width), f32),
+            whole,
+            whole,
+            pltpu.VMEM((FACTORS, 2, 4, blocks, shard, W), bf16),
+            pltpu.VMEM((FACTORS, 4, blocks, shard, W), bf16),
+            pltpu.VMEM((FACTORS, 4, blocks, shard, W), bf16),
+            pltpu.VMEM((FACTORS, 3, blocks, shard, W), bf16),
+            pltpu.VMEM((FACTORS, blocks, shard, W), f32),
+            dma((FACTORS,)),
+            dma((2 + FACTORS,)),
+            dma((4, CHUNKS)),
+            dma((4, CHUNKS)),
+            dma((FACTORS,)),
+            dma((FACTORS,)),
+            dma((FACTORS, 3)),
+            dma((FACTORS, 3)),
+        ],
+        compiler_params=pltpu.CompilerParams(
+            collective_id=0, has_side_effects=True, vmem_limit_bytes=48 * 1024 * 1024
+        ),
+        name="butterfly",
+    )(tokens, upstream, w)
+    return activated, token_grad, weight_grad.transpose(2, 1, 0, 3)
+
+
+def on_device(tokens, weights, upstream):
+    blocks = tokens.shape[1] // BLOCK_FEATURES
+    fits = (
+        lax.axis_size("dp") == 8
+        and lax.axis_size("tensor") == 4
+        and blocks == 4
+        and tokens.shape[0] % (16 * CHUNKS) == 0
+        and tokens.shape[0] <= 256
+    )
+    if fits:
+        return fused_device(tokens, weights, upstream)
+    return plain_device(tokens, weights, upstream)
+
+
 def solution(mesh):
     placed = (P("dp", "tensor"), P(None, "tensor", None, None), P("dp", "tensor"))
     return jax.shard_map(

time: 289 us -> 90 us (0.31)
  waiting for transfers between devices: 160 us -> 0 us
  Pallas kernels: 0 us -> 80.3 us
  local copies, waits for them, and re-layouts: 78.8 us -> 8.92 us
  matrix products: 23.9 us -> 0 us
  between operations: 15 us -> 0.66 us
  starting transfers between devices: 6.02 us -> 0 us
  other arithmetic: 4.02 us -> 0 us
    unnamed x2 -> x0, waiting for transfers between devices: 122 us -> none
    pallas_call x0 -> x1, Pallas kernels: none -> 80.3 us  [fused_device(): pl.pallas_call(functools.partial(fused_kernel, scale_factor), out_shape=(...]
    ppermute x4 -> x0, waiting for transfers between devices: 38.9 us -> none  [partner_2(): return lax.ppermute(block, axis, route)]
    slice x2 -> x0, local copies, waits for them, and re-layouts: 30.9 us -> none  [the longest x1 16 us: on_device(): factor_weight[:BLOCK_FEATURES]]
    dot_general x16 -> x0, matrix products: 23.9 us -> none  [the longest x4 11.1 us: on_device(): jnp.einsum('hjk,kjg->hjg', gathered_input, weights[:, :, factor_matrix, :...]
    unnamed x43 -> x8, local copies, waits for them, and re-layouts: 30.1 us -> 8.92 us
    another operation x3 -> x0, local copies, waits for them, and re-layouts: 12 us -> none  [the longest x1 10.5 us: on_device(): jnp.stack(pieces, axis=2)]
    ppermute x4 -> x0, starting transfers between devices: 5.99 us -> none  [partner_2(): return lax.ppermute(block, axis, route)]
  transfers between devices with their start and end apart: 5 -> 0, of which waited for: 5 -> 0; matrix products, arithmetic and copies ran while one was open for 13% -> 0% of each run, Pallas kernels for 0% -> 0%
where the time goes in v1:
time: 90 us; the launch traced here: 89.9 us
  Pallas kernels  80.3 us (89%)
  local copies, waits for them, and re-layouts  8.92 us (10%)
    pallas_call x1, Pallas kernels, fused_device(): pl.pallas_call(functools.partial(fused_kernel, scale_factor), out_shape=(...  80.3 us
    unnamed x8, local copies, waits for them, and re-layouts  8.92 us

profile of v1, /device:TPU:0, one launch (start us, length us, event | category | flops | bytes accessed | tf_op | source)
XLA Modules:
  0.0 89.9 jit_solution(18149972874396173677)
XLA Ops:
  0.6 0.0 copy-start.1
  0.6 0.0 copy-start
  0.7 5.7 %copy.9 = bf16[512,4,4,256]{3,0,1,2:T(8,128)(2,1)} copy(bf16[512,4,4,256]{3,2,1,0:T(4,128)(2,1)} %param.4) | data formatting | bytes 8388608 | tf_op args[1]
  6.3 0.0 copy-done.1
  6.3 0.0 copy-done
  6.3 80.3 %butterfly.1 = (bf16[256,1024]{1,0:T(8,128)(2,1)S(1)}, bf16[256,1024]{1,0:T(8,128)(2,1)S(1)}, f32[4,4,64,256]{3,2,1,0:T(8,128)S(1)}) custom-call(bf16[256,1024]{1,0:T(8,128)(2,1)S(1)} %copy-done, bf16[256,1024]{1,0:T(8,128)(2,1)S(1)} %copy-done.1, bf16[4,4,512,256]{3,2,1,0:T(8,128)(2,1)} %bitcast.5), custom_call_target="tpu_custom_call" | custom-call | tf_op jit(solution)/shard_map/butterfly/pallas_call | solution.py:393
  86.6 1.6 %copy.7 = f32[64,4,4,256]{3,2,1,0:T(4,128)} copy(f32[64,4,4,256]{3,0,1,2:T(8,128)S(1)} %bitcast.4) | data formatting | bytes 2097152
  88.3 0.8 copy.12
  89.1 0.8 copy.13
Async XLA Ops:
  0.6 5.7 %copy-start.1 = (bf16[256,1024]{1,0:T(8,128)(2,1)S(1)}, bf16[256,1024]{1,0:T(8,128)(2,1)}, u32[]{:S(2)}) copy-start(bf16[256,1024]{1,0:T(8,128)(2,1)} %up_ref.1) | copy-start | bytes 1572868
  0.6 5.7 %copy-start = (bf16[256,1024]{1,0:T(8,128)(2,1)S(1)}, bf16[256,1024]{1,0:T(8,128)(2,1)}, u32[]{:S(2)}) copy-start(bf16[256,1024]{1,0:T(8,128)(2,1)} %tok_ref.1) | copy-start | bytes 1572868

commit v2 on v0

--- a/solution.py
+++ b/solution.py
@@ -1,8 +1,11 @@
+import functools
 import math
 
 import jax
 import jax.numpy as jnp
 from jax import lax
+from jax.experimental import pallas as pl
+from jax.experimental.pallas import tpu as pltpu
 from jax.sharding import PartitionSpec as P
 
 BLOCK_FEATURES = 256
@@ -56,7 +59,7 @@
     )
 
 
-def on_device(tokens, weights, upstream):
+def plain_device(tokens, weights, upstream):
     tok_count = tokens.shape[0]
     blocks = tokens.shape[1] // BLOCK_FEATURES
     scale_factor = 1.0 / math.sqrt(tok_count * lax.axis_size("dp"))
@@ -112,6 +115,417 @@
     return (activated, token_grad, weight_grad)
 
 
+SKEW = 1
+REDO = (3,)
+ORDER = (0, 2, 1, 3)
+MESH = pl.DeviceIdType.MESH
+W = BLOCK_FEATURES
+NN = (((1,), (0,)), ((), ()))
+NT = (((1,), (1,)), ((), ()))
+TN = (((0,), (0,)), ((), ()))
+GELU_A = 0.7978845608
+GELU_B = 0.044715
+
+
+def dot(a, b, dims):
+    return lax.dot_general(a, b, dims, preferred_element_type=jnp.float32)
+
+
+def flip(index, bit):
+    return index + bit - 2 * bit * (lax.rem(index // bit, 2))
+
+
+def fused_kernel(
+    scale_factor,
+    tok_ref,
+    up_ref,
+    w_hbm,
+    act_out,
+    tg_out,
+    wg_out,
+    w,
+    w_far,
+    up_far,
+    z,
+    part,
+    grad,
+    hand,
+    hand_in,
+    self_part,
+    act,
+    tgrad,
+    wg,
+    wg_core,
+    wg_sum,
+    wg_in,
+    wg_fin,
+    w_sem,
+    out_sem,
+    z_send,
+    z_recv,
+    core_send,
+    core_recv,
+    chip_send,
+    chip_recv,
+    far_send,
+    far_recv,
+    share_send,
+    share_recv,
+):
+    rows = tok_ref.shape[0]
+    blocks = tok_ref.shape[1] // W
+    shard = wg_fin.shape[2]
+    dp = lax.axis_index("dp")
+    tensor = lax.axis_index("tensor")
+    core = lax.rem(dp, 2)
+    chip = dp // 2
+
+    loads = []
+    for k in range(FACTORS):
+        load = pltpu.make_async_copy(w_hbm.at[k], w.at[k], w_sem.at[k])
+        load.start()
+        loads.append(load)
+
+    near = (dp, flip(tensor, 1))
+    far = (dp, flip(tensor, 2))
+    sibling = (flip(dp, 1), tensor)
+    chips = [flip(chip, 1), flip(chip, 2), 3 - chip]
+    others = [(2 * c + core, tensor) for c in chips]
+
+    barrier = pltpu.get_barrier_semaphore()
+    peers = [dp]
+    for bit in (1, 2, 4):
+        peers += [flip(p, bit) for p in peers]
+    for device in [near, far] + [(p, tensor) for p in peers[1:]]:
+        pl.semaphore_signal(barrier, inc=1, device_id=device, device_id_type=MESH)
+    pl.semaphore_wait(barrier, 9)
+    mine = pl.ds(pl.multiple_of(dp * shard, shard), shard)
+
+    def far_copy(r, what):
+        i = REDO[r]
+        src = up_ref.at[:, i * W : (i + 1) * W] if what else w_hbm.at[3, i, mine]
+        return pltpu.make_async_remote_copy(
+            src_ref=src,
+            dst_ref=up_far.at[r] if what else w_far.at[r, mine],
+            send_sem=far_send.at[r, what],
+            recv_sem=far_recv.at[r, what],
+            device_id=far,
+            device_id_type=MESH,
+        )
+
+    def share_copy(r, m, sender=None):
+        rows_of = pl.ds(pl.multiple_of((dp if sender is None else sender) * shard, shard), shard)
+        return pltpu.make_async_remote_copy(
+            src_ref=w_far.at[r, rows_of],
+            dst_ref=w_far.at[r, rows_of],
+            send_sem=share_send.at[r, m - 1],
+            recv_sem=share_recv.at[r, m - 1],
+            device_id=(peers[m], tensor),
+            device_id_type=MESH,
+        )
+
+    for what in (0, 1):
+        for r in range(len(REDO)):
+            far_copy(r, what).start()
+
+    def col(i):
+        return slice(i * W, (i + 1) * W)
+
+    def z_copy(stage, i):
+        src = (z.at[2], z.at[3], hand.at[1], hand.at[0])[stage]
+        dst = (part.at[0], part.at[1], hand_in.at[1], hand_in.at[0])[stage]
+        return pltpu.make_async_remote_copy(
+            src_ref=src.at[i],
+            dst_ref=dst.at[i],
+            send_sem=z_send.at[stage, i],
+            recv_sem=z_recv.at[stage, i],
+            device_id=(near, far, far, near)[stage],
+            device_id_type=MESH,
+        )
+
+    def z_value(k, i):
+        return tok_ref[:, col(i)] if k == 0 else z[k, i]
+
+    def partner_value(k, i):
+        return z_value(k, i ^ (1 << k)) if k < 2 else part[k - 2, i]
+
+    def factor(k, i):
+        total = dot(z_value(k, i), w[k, i, :W, :], NN)
+        return (total + dot(partner_value(k, i), w[k, i, W:, :], NN)).astype(jnp.bfloat16)
+
+    def stage_f1(i):
+        z[2, i] = factor(1, i)
+        z_copy(0, i).start()
+
+    def stage_f2(i):
+        z_copy(0, i).wait_recv()
+        z[3, i] = factor(2, i)
+        z_copy(1, i).start()
+
+    def gelu_slope(v):
+        square = v * v
+        t = jnp.tanh(GELU_A * (v + GELU_B * (v * square)))
+        half = 0.5 * (1.0 + t)
+        slope = half + (0.5 * v) * (1.0 - t * t) * (GELU_A * (1.0 + 3.0 * GELU_B * square))
+        return half, slope
+
+    def stage_f3(i):
+        z_copy(1, i).wait_recv()
+        v = factor(3, i).astype(jnp.float32)
+        half, slope = gelu_slope(v)
+        act[:, col(i)] = (v * half).astype(jnp.bfloat16)
+        g = (up_ref[:, col(i)].astype(jnp.float32) * slope).astype(jnp.bfloat16)
+        grad[3, i] = g
+        if i in REDO:
+            r = REDO.index(i)
+            for m in range(1, len(peers)):
+                share_copy(r, m, peers[m]).wait_recv()
+            far_copy(r, 1).wait_recv()
+            v = dot(part[1, i], w_far[r, :W, :], NN) + dot(z[3, i], w_far[r, W:, :], NN)
+            _, slope = gelu_slope(v.astype(jnp.bfloat16).astype(jnp.float32))
+            g = (up_far[r].astype(jnp.float32) * slope).astype(jnp.bfloat16)
+            hand_in[1, i] = dot(g, w_far[r, W:, :], NT).astype(jnp.bfloat16)
+        else:
+            hand[1, i] = dot(g, w[3, i, W:, :], NT).astype(jnp.bfloat16)
+            z_copy(2, i).start()
+        self_part[1, i] = dot(grad[3, i], w[3, i, :W, :], NT)
+        if i in REDO:
+            stage_b3(i)
+        weight_terms(3, i)
+
+    def stage_b3(i):
+        if i not in REDO:
+            z_copy(2, i).wait_recv()
+        g = (self_part[1, i] + hand_in[1, i].astype(jnp.float32)).astype(jnp.bfloat16)
+        grad[2, i] = g
+        hand[0, i] = dot(g, w[2, i, W:, :], NT).astype(jnp.bfloat16)
+        z_copy(3, i).start()
+        self_part[0, i] = dot(grad[2, i], w[2, i, :W, :], NT)
+        weight_terms(2, i)
+
+    def stage_b2(i):
+        z_copy(3, i).wait_recv()
+        g = self_part[0, i] + hand_in[0, i].astype(jnp.float32)
+        grad[1, i] = g.astype(jnp.bfloat16)
+        weight_terms(1, i)
+
+    def stage_local(k, i, j):
+        both = {m: dot(grad[k, m], w[k, m], NT) for m in (i, j)}
+        for m, n in ((i, j), (j, i)):
+            handed = both[n][:, W:].astype(jnp.bfloat16).astype(jnp.float32)
+            g = (both[m][:, :W] + handed).astype(jnp.bfloat16)
+            if k == 1:
+                grad[0, m] = g
+            else:
+                tgrad[:, col(m)] = g
+
+    def core_copy(k, i):
+        return pltpu.make_async_remote_copy(
+            src_ref=wg.at[k, i, 1 - core],
+            dst_ref=wg_core.at[k, i],
+            send_sem=core_send.at[k, i],
+            recv_sem=core_recv.at[k, i],
+            device_id=sibling,
+            device_id_type=MESH,
+        )
+
+    def chip_copy(k, i, m):
+        return pltpu.make_async_remote_copy(
+            src_ref=wg_sum.at[k, i, chips[m]],
+            dst_ref=wg_in.at[k, i, m],
+            send_sem=chip_send.at[k, i, m],
+            recv_sem=chip_recv.at[k, i, m],
+            device_id=others[m],
+            device_id_type=MESH,
+        )
+
+    def weight_terms(k, i):
+        per = W // shard
+        g = grad[k, i]
+        for side, left in enumerate((z_value(k, i), partner_value(k, i))):
+            total = dot(left, g, TN).astype(jnp.bfloat16)
+            for j in range(per):
+                at = side * per + j
+                wg[k, i, at % 2, at // 2] = total[j * shard : (j + 1) * shard]
+        core_copy(k, i).start()
+
+    def weight_sum(k, i):
+        core_copy(k, i).wait_recv()
+        kept = wg[k, i, core].astype(jnp.float32)
+        wg_sum[k, i] = (kept + wg_core[k, i].astype(jnp.float32)).astype(jnp.bfloat16)
+        for m in (2, 0, 1):
+            chip_copy(k, i, m).start()
+
+    def weight_final(k, i):
+        total = wg_sum[k, i, chip].astype(jnp.float32)
+        for m in range(3):
+            chip_copy(k, i, m).wait_recv()
+            total = total + wg_in[k, i, m].astype(jnp.float32)
+        wg_fin[k, i] = total * scale_factor
+
+    outs = []
+
+    def store(src, dst, slot):
+        outs.append(pltpu.make_async_copy(src, dst, out_sem.at[slot]))
+        outs[-1].start()
+
+    loads[0].wait()
+    for i in range(blocks):
+        z[1, i] = factor(0, i)
+    for load in loads[1:]:
+        load.wait()
+
+    order = ORDER
+    work = []
+    for p, i in enumerate(order):
+        for stage, run in enumerate((stage_f1, stage_f2, stage_f3, stage_b3, stage_b2)):
+            if i in REDO and run is stage_b3:
+                continue
+            work.append((p + SKEW * stage, -stage, functools.partial(run, i)))
+        for k, stage in ((3, 2), (2, 3)):
+            work.append((p + SKEW * stage + 1, 1, functools.partial(weight_sum, k, i)))
+    def share():
+        for r in range(len(REDO)):
+            far_copy(r, 0).wait_recv()
+            for m in (6, 7, 2, 3, 4, 5, 1):
+                share_copy(r, m).start()
+
+    work.append((1, 1, functools.partial(share)))
+    for _, _, run in sorted(work, key=lambda item: item[:2]):
+        if run.func is stage_b2 and run.args[0] == 1:
+            store(act, act_out, 0)
+            stage_local(1, 0, 2)
+            weight_terms(0, 0)
+            weight_terms(0, 2)
+            weight_sum(1, 0)
+            weight_sum(1, 2)
+        run()
+        if run.func is stage_b2 and run.args[0] == 1:
+            weight_sum(0, 0)
+            weight_sum(0, 2)
+    stage_local(1, 1, 3)
+    weight_terms(0, 1)
+    weight_terms(0, 3)
+    for k, i in ((1, 1), (1, 3), (0, 1), (0, 3)):
+        weight_sum(k, i)
+    stage_local(0, 0, 1)
+    stage_local(0, 2, 3)
+    store(tgrad, tg_out, 1)
+    for k in (3, 2, 1, 0):
+        for i in order:
+            weight_final(k, i)
+        store(wg_fin.at[k], wg_out.at[k], 2 + k)
+    for i in range(blocks):
+        for stage in range(4):
+            if stage != 2 or i not in REDO:
+                z_copy(stage, i).wait_send()
+        for k in range(FACTORS):
+            core_copy(k, i).wait_send()
+            for m in range(3):
+                chip_copy(k, i, m).wait_send()
+    for r in range(len(REDO)):
+        for what in (0, 1):
+            far_copy(r, what).wait_send()
+        for m in range(1, len(peers)):
+            share_copy(r, m).wait_send()
+    for copy in outs:
+        copy.wait()
+
+
+def finish_kernel(act_ref, tg_ref, wg_ref, act_out, tg_out, wg_out):
+    act_out[...] = act_ref[...]
+    tg_out[...] = tg_ref[...]
+    for k in range(FACTORS):
+        for i in range(wg_ref.shape[1]):
+            wg_out[:, i, k, :] = wg_ref[k, i]
+
+
+def fused_device(tokens, weights, upstream):
+    rows, width = tokens.shape
+    blocks = width // W
+    dp = lax.axis_size("dp")
+    shard = 2 * W // dp
+    scale_factor = 1.0 / math.sqrt(rows * dp)
+    w = weights.transpose(2, 1, 0, 3)
+    bf16, f32 = jnp.bfloat16, jnp.float32
+    dma = pltpu.SemaphoreType.DMA
+    whole = pltpu.VMEM((rows, width), bf16)
+    activated, token_grad, weight_grad = pl.pallas_call(
+        functools.partial(fused_kernel, scale_factor),
+        out_shape=(
+            jax.ShapeDtypeStruct((rows, width), bf16),
+            jax.ShapeDtypeStruct((rows, width), bf16),
+            jax.ShapeDtypeStruct((FACTORS, blocks, shard, W), f32),
+        ),
+        in_specs=[
+            pl.BlockSpec(memory_space=pltpu.VMEM),
+            pl.BlockSpec(memory_space=pltpu.VMEM),
+            pl.BlockSpec(memory_space=pl.ANY),
+        ],
+        out_specs=[pl.BlockSpec(memory_space=pl.ANY)] * 3,
+        scratch_shapes=[
+            pltpu.VMEM((FACTORS, blocks, 2 * W, W), bf16),
+            pltpu.VMEM((len(REDO), 2 * W, W), bf16),
+            pltpu.VMEM((len(REDO), rows, W), bf16),
+            pltpu.VMEM((4, blocks, rows, W), bf16),
+            pltpu.VMEM((2, blocks, rows, W), bf16),
+            pltpu.VMEM((4, blocks, rows, W), bf16),
+            pltpu.VMEM((2, blocks, rows, W), bf16),
+            pltpu.VMEM((2, blocks, rows, W), bf16),
+            pltpu.VMEM((2, blocks, rows, W), f32),
+            whole,
+            whole,
+            pltpu.VMEM((FACTORS, blocks, 2, 4, shard, W), bf16),
+            pltpu.VMEM((FACTORS, blocks, 4, shard, W), bf16),
+            pltpu.VMEM((FACTORS, blocks, 4, shard, W), bf16),
+            pltpu.VMEM((FACTORS, blocks, 3, shard, W), bf16),
+            pltpu.VMEM((FACTORS, blocks, shard, W), f32),
+            dma((FACTORS,)),
+            dma((2 + FACTORS,)),
+            dma((4, blocks)),
+            dma((4, blocks)),
+            dma((FACTORS, blocks)),
+            dma((FACTORS, blocks)),
+            dma((FACTORS, blocks, 3)),
+            dma((FACTORS, blocks, 3)),
+            dma((len(REDO), 2)),
+            dma((len(REDO), 2)),
+            dma((len(REDO), 7)),
+            dma((len(REDO), 7)),
+        ],
+        compiler_params=pltpu.CompilerParams(
+            collective_id=0, has_side_effects=True, vmem_limit_bytes=48 * 1024 * 1024
+        ),
+        name="butterfly",
+    )(tokens, upstream, w)
+    return pl.pallas_call(
+        finish_kernel,
+        out_shape=(
+            jax.ShapeDtypeStruct((rows, width), bf16),
+            jax.ShapeDtypeStruct((rows, width), bf16),
+            jax.ShapeDtypeStruct((shard, blocks, FACTORS, W), f32),
+        ),
+        in_specs=[pl.BlockSpec(memory_space=pltpu.VMEM)] * 3,
+        out_specs=[pl.BlockSpec(memory_space=pltpu.VMEM)] * 3,
+        compiler_params=pltpu.CompilerParams(vmem_limit_bytes=16 * 1024 * 1024),
+        name="finish",
+    )(activated, token_grad, weight_grad)
+
+
+def on_device(tokens, weights, upstream):
+    blocks = tokens.shape[1] // BLOCK_FEATURES
+    fits = (
+        lax.axis_size("dp") == 8
+        and lax.axis_size("tensor") == 4
+        and blocks == 4
+        and tokens.shape[0] % 16 == 0
+        and tokens.shape[0] <= 256
+    )
+    if fits:
+        return fused_device(tokens, weights, upstream)
+    return plain_device(tokens, weights, upstream)
+
+
 def solution(mesh):
     placed = (P("dp", "tensor"), P(None, "tensor", None, None), P("dp", "tensor"))
     return jax.shard_map(

time: 289 us -> 83.8 us (0.29)
  waiting for transfers between devices: 160 us -> 0 us
  Pallas kernels: 0 us -> 77.3 us
  local copies, waits for them, and re-layouts: 78.8 us -> 5.69 us
  matrix products: 23.9 us -> 0 us
  between operations: 15 us -> 0.66 us
  starting transfers between devices: 6.02 us -> 0 us
  other arithmetic: 4.02 us -> 0 us
    unnamed x2 -> x0, waiting for transfers between devices: 122 us -> none
    pallas_call x0 -> x2, Pallas kernels: none -> 77.3 us  [the longest x1 75.5 us: fused_device(): pl.pallas_call(functools.partial(fused_kernel, scale_factor), out_shape=(...]
    ppermute x4 -> x0, waiting for transfers between devices: 38.9 us -> none  [partner_2(): return lax.ppermute(block, axis, route)]
    slice x2 -> x0, local copies, waits for them, and re-layouts: 30.9 us -> none  [the longest x1 16 us: on_device(): factor_weight[:BLOCK_FEATURES]]
    unnamed x43 -> x5, local copies, waits for them, and re-layouts: 30.1 us -> 5.69 us
    dot_general x16 -> x0, matrix products: 23.9 us -> none  [the longest x4 11.1 us: on_device(): jnp.einsum('hjk,kjg->hjg', gathered_input, weights[:, :, factor_matrix, :...]
    another operation x3 -> x0, local copies, waits for them, and re-layouts: 12 us -> none  [the longest x1 10.5 us: on_device(): jnp.stack(pieces, axis=2)]
    ppermute x4 -> x0, starting transfers between devices: 5.99 us -> none  [partner_2(): return lax.ppermute(block, axis, route)]
  transfers between devices with their start and end apart: 5 -> 0, of which waited for: 5 -> 0; matrix products, arithmetic and copies ran while one was open for 13% -> 0% of each run, Pallas kernels for 0% -> 0%
where the time goes in v2:
time: 83.8 us; the launch traced here: 83.6 us
  Pallas kernels  77.3 us (92%)
  local copies, waits for them, and re-layouts  5.69 us (7%)
    pallas_call x1, Pallas kernels, fused_device(): pl.pallas_call(functools.partial(fused_kernel, scale_factor), out_shape=(...  75.5 us
    unnamed x5, local copies, waits for them, and re-layouts  5.69 us
    pallas_call x1, Pallas kernels, fused_device(): pl.pallas_call(finish_kernel, out_shape=(jax.ShapeDtypeStruct((rows, widt...  1.77 us

profile of v2, /device:TPU:0, one launch (start us, length us, event | category | flops | bytes accessed | tf_op | source)
XLA Modules:
  0.0 83.6 jit_solution(17441644168582791254)
XLA Ops:
  0.6 0.0 copy-start.1
  0.6 0.0 copy-start
  0.7 5.7 %copy.8 = bf16[512,4,4,256]{3,0,1,2:T(8,128)(2,1)} copy(bf16[512,4,4,256]{3,2,1,0:T(4,128)(2,1)} %param.4) | data formatting | bytes 8388608 | tf_op args[1]
  6.3 0.0 copy-done.1
  6.3 0.0 copy-done
  6.3 75.5 %butterfly.1 = (bf16[256,1024]{1,0:T(8,128)(2,1)S(1)}, bf16[256,1024]{1,0:T(8,128)(2,1)S(1)}, f32[4,4,64,256]{3,2,1,0:T(8,128)S(1)}) custom-call(bf16[256,1024]{1,0:T(8,128)(2,1)S(1)} %copy-done, bf16[256,1024]{1,0:T(8,128)(2,1)S(1)} %copy-done.1, bf16[4,4,512,256]{3,2,1,0:T(8,128)(2,1)} %bitcast.3), custom_call_target="tpu_custom_call" | custom-call | tf_op jit(solution)/shard_map/butterfly/pallas_call | solution.py:453
  81.9 1.8 %finish.1 = (bf16[256,1024]{1,0:T(8,128)(2,1)}, bf16[256,1024]{1,0:T(8,128)(2,1)}, f32[64,4,4,256]{3,2,1,0:T(4,128)}) custom-call(bf16[256,1024]{1,0:T(8,128)(2,1)S(1)} %get-tuple-element.6.act_ref, bf16[256,1024]{1,0:T(8,128)(2,1)S(1)} %get-tuple-element.7.tg_ref, f32[4,4,64,256]{3,2,1,0:T(8,128)S(1)} %get-tuple-element.8.wg_ref), custom_call_target="tpu_custom_call" | custom-call | tf_op jit(solution)/shard_map/finish/pallas_call | solution.py:501
Async XLA Ops:
  0.6 5.7 %copy-start.1 = (bf16[256,1024]{1,0:T(8,128)(2,1)S(1)}, bf16[256,1024]{1,0:T(8,128)(2,1)}, u32[]{:S(2)}) copy-start(bf16[256,1024]{1,0:T(8,128)(2,1)} %up_ref.1) | copy-start | bytes 1572868
  0.6 5.7 %copy-start = (bf16[256,1024]{1,0:T(8,128)(2,1)S(1)}, bf16[256,1024]{1,0:T(8,128)(2,1)}, u32[]{:S(2)}) copy-start(bf16[256,1024]{1,0:T(8,128)(2,1)} %tok_ref.1) | copy-start | bytes 1572868

commit v3 on v2

--- a/solution.py
+++ b/solution.py
@@ -115,7 +115,7 @@
     return (activated, token_grad, weight_grad)
 
 
-SKEW = 1
+SKEW = 2
 REDO = (3,)
 ORDER = (0, 2, 1, 3)
 MESH = pl.DeviceIdType.MESH
@@ -139,11 +139,10 @@
     scale_factor,
     tok_ref,
     up_ref,
-    w_hbm,
+    w,
     act_out,
     tg_out,
     wg_out,
-    w,
     w_far,
     up_far,
     z,
@@ -159,7 +158,6 @@
     wg_sum,
     wg_in,
     wg_fin,
-    w_sem,
     out_sem,
     z_send,
     z_recv,
@@ -180,12 +178,6 @@
     core = lax.rem(dp, 2)
     chip = dp // 2
 
-    loads = []
-    for k in range(FACTORS):
-        load = pltpu.make_async_copy(w_hbm.at[k], w.at[k], w_sem.at[k])
-        load.start()
-        loads.append(load)
-
     near = (dp, flip(tensor, 1))
     far = (dp, flip(tensor, 2))
     sibling = (flip(dp, 1), tensor)
@@ -203,7 +195,7 @@
 
     def far_copy(r, what):
         i = REDO[r]
-        src = up_ref.at[:, i * W : (i + 1) * W] if what else w_hbm.at[3, i, mine]
+        src = up_ref.at[:, i * W : (i + 1) * W] if what else w.at[3, i, mine]
         return pltpu.make_async_remote_copy(
             src_ref=src,
             dst_ref=up_far.at[r] if what else w_far.at[r, mine],
@@ -231,36 +223,41 @@
     def col(i):
         return slice(i * W, (i + 1) * W)
 
-    def z_copy(stage, i):
+    half_rows = rows // 2
+
+    def half_of(h):
+        return slice(h * half_rows, (h + 1) * half_rows)
+
+    def z_copy(stage, i, h):
         src = (z.at[2], z.at[3], hand.at[1], hand.at[0])[stage]
         dst = (part.at[0], part.at[1], hand_in.at[1], hand_in.at[0])[stage]
         return pltpu.make_async_remote_copy(
-            src_ref=src.at[i],
-            dst_ref=dst.at[i],
-            send_sem=z_send.at[stage, i],
-            recv_sem=z_recv.at[stage, i],
+            src_ref=src.at[i, pl.ds(h * half_rows, half_rows)],
+            dst_ref=dst.at[i, pl.ds(h * half_rows, half_rows)],
+            send_sem=z_send.at[stage, i, h],
+            recv_sem=z_recv.at[stage, i, h],
             device_id=(near, far, far, near)[stage],
             device_id_type=MESH,
         )
 
-    def z_value(k, i):
-        return tok_ref[:, col(i)] if k == 0 else z[k, i]
-
-    def partner_value(k, i):
-        return z_value(k, i ^ (1 << k)) if k < 2 else part[k - 2, i]
-
-    def factor(k, i):
-        total = dot(z_value(k, i), w[k, i, :W, :], NN)
-        return (total + dot(partner_value(k, i), w[k, i, W:, :], NN)).astype(jnp.bfloat16)
-
-    def stage_f1(i):
-        z[2, i] = factor(1, i)
-        z_copy(0, i).start()
-
-    def stage_f2(i):
-        z_copy(0, i).wait_recv()
-        z[3, i] = factor(2, i)
-        z_copy(1, i).start()
+    def z_value(k, i, at=slice(None)):
+        return tok_ref[at, col(i)] if k == 0 else z[k, i, at]
+
+    def partner_value(k, i, at=slice(None)):
+        return z_value(k, i ^ (1 << k), at) if k < 2 else part[k - 2, i, at]
+
+    def factor(k, i, at=slice(None)):
+        total = dot(z_value(k, i, at), w[k, i, :W, :], NN)
+        return (total + dot(partner_value(k, i, at), w[k, i, W:, :], NN)).astype(jnp.bfloat16)
+
+    def stage_f1(i, h):
+        z[2, i, half_of(h)] = factor(1, i, half_of(h))
+        z_copy(0, i, h).start()
+
+    def stage_f2(i, h):
+        z_copy(0, i, h).wait_recv()
+        z[3, i, half_of(h)] = factor(2, i, half_of(h))
+        z_copy(1, i, h).start()
 
     def gelu_slope(v):
         square = v * v
@@ -269,45 +266,52 @@
         slope = half + (0.5 * v) * (1.0 - t * t) * (GELU_A * (1.0 + 3.0 * GELU_B * square))
         return half, slope
 
-    def stage_f3(i):
-        z_copy(1, i).wait_recv()
-        v = factor(3, i).astype(jnp.float32)
+    def stage_f3(i, h):
+        at = half_of(h)
+        z_copy(1, i, h).wait_recv()
+        v = factor(3, i, at).astype(jnp.float32)
         half, slope = gelu_slope(v)
-        act[:, col(i)] = (v * half).astype(jnp.bfloat16)
-        g = (up_ref[:, col(i)].astype(jnp.float32) * slope).astype(jnp.bfloat16)
-        grad[3, i] = g
+        act[at, col(i)] = (v * half).astype(jnp.bfloat16)
+        g = (up_ref[at, col(i)].astype(jnp.float32) * slope).astype(jnp.bfloat16)
+        grad[3, i, at] = g
         if i in REDO:
             r = REDO.index(i)
-            for m in range(1, len(peers)):
-                share_copy(r, m, peers[m]).wait_recv()
-            far_copy(r, 1).wait_recv()
-            v = dot(part[1, i], w_far[r, :W, :], NN) + dot(z[3, i], w_far[r, W:, :], NN)
+            if h == 0:
+                for m in range(1, len(peers)):
+                    share_copy(r, m, peers[m]).wait_recv()
+                far_copy(r, 1).wait_recv()
+            v = dot(part[1, i, at], w_far[r, :W, :], NN) + dot(z[3, i, at], w_far[r, W:, :], NN)
             _, slope = gelu_slope(v.astype(jnp.bfloat16).astype(jnp.float32))
-            g = (up_far[r].astype(jnp.float32) * slope).astype(jnp.bfloat16)
-            hand_in[1, i] = dot(g, w_far[r, W:, :], NT).astype(jnp.bfloat16)
+            g = (up_far[r, at].astype(jnp.float32) * slope).astype(jnp.bfloat16)
+            hand_in[1, i, at] = dot(g, w_far[r, W:, :], NT).astype(jnp.bfloat16)
         else:
-            hand[1, i] = dot(g, w[3, i, W:, :], NT).astype(jnp.bfloat16)
-            z_copy(2, i).start()
-        self_part[1, i] = dot(grad[3, i], w[3, i, :W, :], NT)
+            hand[1, i, at] = dot(g, w[3, i, W:, :], NT).astype(jnp.bfloat16)
+            z_copy(2, i, h).start()
+        self_part[1, i, at] = dot(grad[3, i, at], w[3, i, :W, :], NT)
         if i in REDO:
-            stage_b3(i)
-        weight_terms(3, i)
-
-    def stage_b3(i):
+            stage_b3(i, h)
+        if h == 1:
+            weight_terms(3, i)
+
+    def stage_b3(i, h):
+        at = half_of(h)
         if i not in REDO:
-            z_copy(2, i).wait_recv()
-        g = (self_part[1, i] + hand_in[1, i].astype(jnp.float32)).astype(jnp.bfloat16)
-        grad[2, i] = g
-        hand[0, i] = dot(g, w[2, i, W:, :], NT).astype(jnp.bfloat16)
-        z_copy(3, i).start()
-        self_part[0, i] = dot(grad[2, i], w[2, i, :W, :], NT)
-        weight_terms(2, i)
-
-    def stage_b2(i):
-        z_copy(3, i).wait_recv()
-        g = self_part[0, i] + hand_in[0, i].astype(jnp.float32)
-        grad[1, i] = g.astype(jnp.bfloat16)
-        weight_terms(1, i)
+            z_copy(2, i, h).wait_recv()
+        g = (self_part[1, i, at] + hand_in[1, i, at].astype(jnp.float32)).astype(jnp.bfloat16)
+        grad[2, i, at] = g
+        hand[0, i, at] = dot(g, w[2, i, W:, :], NT).astype(jnp.bfloat16)
+        z_copy(3, i, h).start()
+        self_part[0, i, at] = dot(grad[2, i, at], w[2, i, :W, :], NT)
+        if h == 1:
+            weight_terms(2, i)
+
+    def stage_b2(i, h):
+        at = half_of(h)
+        z_copy(3, i, h).wait_recv()
+        g = self_part[0, i, at] + hand_in[0, i, at].astype(jnp.float32)
+        grad[1, i, at] = g.astype(jnp.bfloat16)
+        if h == 1:
+            weight_terms(1, i)
 
     def stage_local(k, i, j):
         both = {m: dot(grad[k, m], w[k, m], NT) for m in (i, j)}
@@ -369,21 +373,19 @@
         outs.append(pltpu.make_async_copy(src, dst, out_sem.at[slot]))
         outs[-1].start()
 
-    loads[0].wait()
     for i in range(blocks):
         z[1, i] = factor(0, i)
-    for load in loads[1:]:
-        load.wait()
 
     order = ORDER
     work = []
-    for p, i in enumerate(order):
+    for p, (i, h) in enumerate((i, h) for i in order for h in range(2)):
         for stage, run in enumerate((stage_f1, stage_f2, stage_f3, stage_b3, stage_b2)):
             if i in REDO and run is stage_b3:
                 continue
-            work.append((p + SKEW * stage, -stage, functools.partial(run, i)))
+            work.append((p + SKEW * stage, -stage, functools.partial(run, i, h)))
         for k, stage in ((3, 2), (2, 3)):
-            work.append((p + SKEW * stage + 1, 1, functools.partial(weight_sum, k, i)))
+            if h == 1:
+                work.append((p + SKEW * stage + 1, 1, functools.partial(weight_sum, k, i)))
     def share():
         for r in range(len(REDO)):
             far_copy(r, 0).wait_recv()
@@ -392,7 +394,7 @@
 
     work.append((1, 1, functools.partial(share)))
     for _, _, run in sorted(work, key=lambda item: item[:2]):
-        if run.func is stage_b2 and run.args[0] == 1:
+        if run.func is stage_b2 and run.args == (1, 0):
             store(act, act_out, 0)
             stage_local(1, 0, 2)
             weight_terms(0, 0)
@@ -400,7 +402,7 @@
             weight_sum(1, 0)
             weight_sum(1, 2)
         run()
-        if run.func is stage_b2 and run.args[0] == 1:
+        if run.func is stage_b2 and run.args == (1, 0):
             weight_sum(0, 0)
             weight_sum(0, 2)
     stage_local(1, 1, 3)
@@ -418,7 +420,8 @@
     for i in range(blocks):
         for stage in range(4):
             if stage != 2 or i not in REDO:
-                z_copy(stage, i).wait_send()
+                for h in range(2):
+                    z_copy(stage, i, h).wait_send()
         for k in range(FACTORS):
             core_copy(k, i).wait_send()
             for m in range(3):
@@ -460,11 +463,10 @@
         in_specs=[
             pl.BlockSpec(memory_space=pltpu.VMEM),
             pl.BlockSpec(memory_space=pltpu.VMEM),
-            pl.BlockSpec(memory_space=pl.ANY),
+            pl.BlockSpec(memory_space=pltpu.VMEM),
         ],
         out_specs=[pl.BlockSpec(memory_space=pl.ANY)] * 3,
         scratch_shapes=[
-            pltpu.VMEM((FACTORS, blocks, 2 * W, W), bf16),
             pltpu.VMEM((len(REDO), 2 * W, W), bf16),
             pltpu.VMEM((len(REDO), rows, W), bf16),
             pltpu.VMEM((4, blocks, rows, W), bf16),
@@ -480,10 +482,9 @@
             pltpu.VMEM((FACTORS, blocks, 4, shard, W), bf16),
             pltpu.VMEM((FACTORS, blocks, 3, shard, W), bf16),
             pltpu.VMEM((FACTORS, blocks, shard, W), f32),
-            dma((FACTORS,)),
             dma((2 + FACTORS,)),
-            dma((4, blocks)),
-            dma((4, blocks)),
+            dma((4, blocks, 2)),
+            dma((4, blocks, 2)),
             dma((FACTORS, blocks)),
             dma((FACTORS, blocks)),
             dma((FACTORS, blocks, 3)),
@@ -494,7 +495,7 @@
             dma((len(REDO), 7)),
         ],
         compiler_params=pltpu.CompilerParams(
-            collective_id=0, has_side_effects=True, vmem_limit_bytes=48 * 1024 * 1024
+            collective_id=0, has_side_effects=True, vmem_limit_bytes=40 * 1024 * 1024
         ),
         name="butterfly",
     )(tokens, upstream, w)
@@ -518,7 +519,7 @@
         lax.axis_size("dp") == 8
         and lax.axis_size("tensor") == 4
         and blocks == 4
-        and tokens.shape[0] % 16 == 0
+        and tokens.shape[0] % 32 == 0
         and tokens.shape[0] <= 256
     )
     if fits:

time: 83.8 us -> 81.4 us (0.971)
  local copies, waits for them, and re-layouts: 5.69 us -> 3.76 us
    unnamed x5, local copies, waits for them, and re-layouts: 5.69 us -> 3.76 us
where the time goes in v3:
time: 81.4 us; the launch traced here: 81.3 us
  Pallas kernels  76.8 us (94%)
  local copies, waits for them, and re-layouts  3.76 us (5%)
    pallas_call x1, Pallas kernels, fused_device(): pl.pallas_call(functools.partial(fused_kernel, scale_factor), out_shape=(...  75.1 us
    unnamed x5, local copies, waits for them, and re-layouts  3.76 us
    pallas_call x1, Pallas kernels, fused_device(): pl.pallas_call(finish_kernel, out_shape=(jax.ShapeDtypeStruct((rows, widt...  1.77 us

profile of v3, /device:TPU:0, one launch (start us, length us, event | category | flops | bytes accessed | tf_op | source)
XLA Modules:
  0.0 81.3 jit_solution(1500169171816095004)
XLA Ops:
  0.6 0.0 copy-start.1
  0.6 0.0 copy-start
  0.7 3.7 %copy.8 = bf16[512,4,4,256]{3,0,1,2:T(8,128)(2,1)S(1)} copy(bf16[512,4,4,256]{3,2,1,0:T(4,128)(2,1)} %param.4) | data formatting | bytes 8388608 | tf_op args[1]
  4.4 0.0 copy-done.1
  4.4 0.0 copy-done
  4.4 75.1 %butterfly.1 = (bf16[256,1024]{1,0:T(8,128)(2,1)S(1)}, bf16[256,1024]{1,0:T(8,128)(2,1)S(1)}, f32[4,4,64,256]{3,2,1,0:T(8,128)S(1)}) custom-call(bf16[256,1024]{1,0:T(8,128)(2,1)S(1)} %copy-done, bf16[256,1024]{1,0:T(8,128)(2,1)S(1)} %copy-done.1, bf16[4,4,512,256]{3,2,1,0:T(8,128)(2,1)S(1)} %bitcast.3), custom_call_target="tpu_custom_call" | custom-call | tf_op jit(solution)/shard_map/butterfly/pallas_call | solution.py:456
  79.5 1.8 %finish.1 = (bf16[256,1024]{1,0:T(8,128)(2,1)}, bf16[256,1024]{1,0:T(8,128)(2,1)}, f32[64,4,4,256]{3,2,1,0:T(4,128)}) custom-call(bf16[256,1024]{1,0:T(8,128)(2,1)S(1)} %get-tuple-element.6.act_ref, bf16[256,1024]{1,0:T(8,128)(2,1)S(1)} %get-tuple-element.7.tg_ref, f32[4,4,64,256]{3,2,1,0:T(8,128)S(1)} %get-tuple-element.8.wg_ref), custom_call_target="tpu_custom_call" | custom-call | tf_op jit(solution)/shard_map/finish/pallas_call | solution.py:502
Async XLA Ops:
  0.6 3.8 %copy-start.1 = (bf16[256,1024]{1,0:T(8,128)(2,1)S(1)}, bf16[256,1024]{1,0:T(8,128)(2,1)}, u32[]{:S(2)}) copy-start(bf16[256,1024]{1,0:T(8,128)(2,1)} %up_ref.1) | copy-start | bytes 1572868
  0.6 3.8 %copy-start = (bf16[256,1024]{1,0:T(8,128)(2,1)S(1)}, bf16[256,1024]{1,0:T(8,128)(2,1)}, u32[]{:S(2)}) copy-start(bf16[256,1024]{1,0:T(8,128)(2,1)} %tok_ref.1) | copy-start | bytes 1572868
